TPU v7x, 768 devices: a whole 4x8x12 slice. The times are simulated.
768 devices in a mesh: node: 8 (over y_hi, x), span: 96 (over y_lo, z, core).
Axes of the slice: x: 4, y: 8 (y_hi: 2, y_lo: 4; y = y_hi * 4 + y_lo), z: 12, core: 2. Of those that a mesh axis runs over, the one named last changes fastest.
Arguments:
- iterate: float32 [8, 2, 576, 4608], P('node', None, None, 'span'), may hold values from -6 to 6
- start_field: float32 [2, 576, 4608], P(None, None, 'span'), may hold values from -6 to 6
- spanwise_velocity: float32 [8, 576, 4608], P('node', 'span'), may hold values from -6 to 6
- eigen_basis: float32 [576, 576], replicated, may hold values from -3 to 3
- inverse_basis: float32 [576, 576], replicated, may hold values from -3 to 3, as said below
- decay_rates: float32 [576], replicated, may hold values from 0.05 to 5
Outputs:
- updated: float32 [8, 2, 576, 4608], P('node', None, None, 'span')
Inputs may be any that keep to these rules, and one draw needn't show every extreme that they name: inverse_basis is the inverse of eigen_basis up to float32 rounding.
All inputs are finite; a program needn't handle non-finite values.
Results may differ from a plain program's by a relative error of at most 0.00054.
Values may be sent and summed in bfloat16 or wider, within the bound.
A program may use at most 64 MiB of HBM per device.

v0:
```python
import math

import jax
import jax.numpy as jnp
from jax import lax
from jax.sharding import Mesh
from jax.sharding import PartitionSpec as P

NZ = 4608
SPAN = ("span_0", "span_1", "span_2")


def cut_along(shard, dim, devices):
    before, after = (shard.shape[:dim], shard.shape[dim + 1 :])
    return jnp.moveaxis(shard.reshape(*before, devices, -1, *after), dim, 0)


def in_order(pieces, dim):
    pieces = jnp.moveaxis(pieces, 0, dim)
    dims = pieces.shape
    return pieces.reshape(*dims[:dim], dims[dim] * dims[dim + 1], *dims[dim + 2 :])


def turned_blocks(pieces, axes, sequence):
    inside = pieces.shape[1:]
    out = pieces.reshape(*(lax.axis_size(a) for a in axes), *inside)
    for k in sequence:
        out = lax.all_to_all(out, axes[k], k, k, tiled=True)
    return out.reshape(-1, *inside)


def core_and_chips(shard, groups, sequence, split_dim, concat_dim):
    devices = lax.axis_size(groups[0]) * lax.axis_size(groups[1])
    pieces = cut_along(shard, split_dim, devices)
    return in_order(turned_blocks(pieces, groups, sequence), concat_dim)


def collocation(node_total):
    points = [
        0.5 - 0.5 * math.cos((2.0 * m + 1.0) * math.pi / (2.0 * node_total))
        for m in range(node_total)
    ]
    weights = [[0.0] * node_total for _ in range(node_total)]
    for column in range(node_total):
        coeffs = [1.0]
        scale = 1.0
        for other in range(node_total):
            if other != column:
                grown = [0.0] * (len(coeffs) + 1)
                for power in range(len(coeffs)):
                    grown[power + 1] += coeffs[power]
                    grown[power] -= points[other] * coeffs[power]
                coeffs = grown
                scale = scale * (points[column] - points[other])
        for row in range(node_total):
            total = 0.0
            for power in range(len(coeffs)):
                total += coeffs[power] * points[row] ** (power + 1) / (power + 1)
            weights[row][column] = total / scale
    return (weights, [value / node_total for value in points])


def dft_pair(length, direction):
    counter = jnp.arange(length, dtype=jnp.int32)
    phases = (counter[:, None] * counter[None, :] % length).astype(jnp.float32) * (
        2.0 * math.pi / length
    )
    return (jnp.cos(phases), direction * jnp.sin(phases))


def twist_pair(low_factor, high_factor, direction):
    full_length = low_factor * high_factor
    low_counter = jnp.arange(low_factor, dtype=jnp.int32)
    high_counter = jnp.arange(high_factor, dtype=jnp.int32)
    phases = (low_counter[:, None] * high_counter[None, :] % full_length).astype(jnp.float32) * (
        2.0 * math.pi / full_length
    )
    return (jnp.cos(phases), direction * jnp.sin(phases))


def spanwise_transform(real_part, imaginary_part, direction):
    highest = lax.Precision.HIGHEST
    full_length = real_part.shape[-1]
    low_factor = 1
    for candidate in range(1, math.isqrt(full_length) + 1):
        if full_length % candidate == 0:
            low_factor = candidate
    high_factor = full_length // low_factor
    leading = real_part.shape[:-1]
    real_grid = real_part.reshape(leading + (high_factor, low_factor))
    imaginary_grid = imaginary_part.reshape(leading + (high_factor, low_factor))
    cos_high, sin_high = dft_pair(high_factor, direction)
    first_real = jnp.einsum("...rp,rk->...pk", real_grid, cos_high, precision=highest) - jnp.einsum(
        "...rp,rk->...pk", imaginary_grid, sin_high, precision=highest
    )
    first_imaginary = jnp.einsum(
        "...rp,rk->...pk", real_grid, sin_high, precision=highest
    ) + jnp.einsum("...rp,rk->...pk", imaginary_grid, cos_high, precision=highest)
    twist_cos, twist_sin = twist_pair(low_factor, high_factor, direction)
    turned_real = first_real * twist_cos - first_imaginary * twist_sin
    turned_imaginary = first_real * twist_sin + first_imaginary * twist_cos
    cos_low, sin_low = dft_pair(low_factor, direction)
    final_real = jnp.einsum(
        "qp,...pk->...qk", cos_low, turned_real, precision=highest
    ) - jnp.einsum("qp,...pk->...qk", sin_low, turned_imaginary, precision=highest)
    final_imaginary = jnp.einsum(
        "qp,...pk->...qk", sin_low, turned_real, precision=highest
    ) + jnp.einsum("qp,...pk->...qk", cos_low, turned_imaginary, precision=highest)
    normalizer = 1.0 / math.sqrt(full_length)
    return (
        final_real.reshape(leading + (full_length,)) * normalizer,
        final_imaginary.reshape(leading + (full_length,)) * normalizer,
    )


def eigen_apply(matrix, fields):
    return jnp.einsum("yx,mcxq->mcyq", matrix, fields, precision=lax.Precision.HIGHEST)


def local(iterate, start_field, spanwise_velocity, eigen_basis, inverse_basis, decay_rates):
    node_total = lax.axis_size("node") * iterate.shape[0]
    quadrature_table, shift_table = collocation(node_total)
    quadrature = jnp.asarray(quadrature_table, jnp.float32)
    node_index = lax.axis_index("node")
    node_shift = lax.dynamic_index_in_dim(
        jnp.asarray(shift_table, jnp.float32), node_index, 0, keepdims=False
    )
    local_modes = iterate.shape[3]
    wavenumber = lax.axis_index(SPAN) * local_modes + jnp.arange(local_modes, dtype=jnp.int32)
    signed = jnp.where(wavenumber < NZ // 2, wavenumber, wavenumber - NZ).astype(jnp.float32) / (
        NZ // 2
    )
    damping = decay_rates[:, None] + signed[None, :] ** 2
    gradient = jnp.stack([-signed * iterate[:, 1], signed * iterate[:, 0]], axis=1).astype(
        jnp.bfloat16
    )
    span_lines = lax.all_to_all(gradient, SPAN, split_axis=2, concat_axis=3, tiled=True)
    physical_real, physical_imaginary = spanwise_transform(
        span_lines[:, 0].astype(jnp.float32), span_lines[:, 1].astype(jnp.float32), 1.0
    )
    spectral_real, spectral_imaginary = spanwise_transform(
        -spanwise_velocity * physical_real, -spanwise_velocity * physical_imaginary, -1.0
    )
    advect = jnp.stack([spectral_real, spectral_imaginary], axis=1).astype(jnp.bfloat16)
    wall_terms = core_and_chips(advect, (("span_0", "span_1"), "span_2"), (1, 0), 3, 2)
    projected = eigen_apply(inverse_basis, jnp.concatenate([start_field[None], iterate], axis=0))
    section_term = -damping * projected[1:] + eigen_apply(
        inverse_basis, wall_terms.astype(jnp.float32)
    )
    node_major = lax.all_to_all(section_term, "node", split_axis=3, concat_axis=0, tiled=True)
    blended = jnp.einsum("mj,jcyq->mcyq", quadrature, node_major, precision=lax.Precision.HIGHEST)
    summed = lax.all_to_all(blended, "node", split_axis=0, concat_axis=3, tiled=True)[0]
    shifted = node_shift * damping
    new_coeff = (projected[0] + summed + shifted * projected[1]) / (1.0 + shifted)
    return eigen_apply(eigen_basis, new_coeff[None])


def solution(mesh):
    torus = Mesh(
        mesh.devices.reshape(mesh.shape["node"], 4, 12, 2), ("node", "span_0", "span_1", "span_2")
    )
    placed = (
        P("node", None, None, SPAN),
        P(None, None, SPAN),
        P("node", SPAN, None),
        P(),
        P(),
        P(),
    )
    return jax.shard_map(
        local, mesh=torus, in_specs=placed, out_specs=P("node", None, None, SPAN), check_vma=False
    )
```

profile of v0, /device:TPU:8, one launch (start us, length us, event | category | flops | bytes accessed | tf_op | source)
XLA Modules:
  0.0 111.3 jit_solution(7047468966477183154)
XLA Ops:
  0.0 1.2 %multiply_convert_fusion.1 = (bf16[1,1,576,48]{2,3,1,0:T(8,128)(2,1)S(1)}, bf16[1,1,576,48]{2,3,1,0:T(8,128)(2,1)S(1)}) fusion(f32[1,2,576,48]{2,3,1,0:T(8,128)} %param.8, f32[48]{0:T(128)S(1)} %get-tuple-element.15, f32[48]{0:T(128)S(1)} %get-tuple-element.14), kind=kLoop, calls=%fused_computation.53 | loop fusion | flops 110592 | bytes 332160 | tf_op jit(solution)/shard_map/convert.8
  1.4 1.1 reshape.447
  2.5 19.6 %all-to-all-start = ((bf16[96,2,288]{2,1,0:T(2,128)(2,1)}), bf16[96,2,288]{2,1,0:T(2,128)(2,1)S(1)}, u32[]{:S(2)}, u32[]{:S(2)}) async-start(bf16[96,2,288]{2,1,0:T(2,128)(2,1)} %reshape.447), calls=%async_computation | async-start | bytes 294912 | tf_op jit(solution)/shard_map/all_to_all | solution.py:137
  22.1 0.7 dynamic_slice.4
  23.1 14.1 %all-to-all-done = bf16[96,2,288]{2,1,0:T(2,128)(2,1)S(1)} async-done(((bf16[96,2,288]{2,1,0:T(2,128)(2,1)}), bf16[96,2,288]{2,1,0:T(2,128)(2,1)S(1)}, u32[]{:S(2)}, u32[]{:S(2)}) %all-to-all-start) | async-done | bytes 110624 | tf_op jit(solution)/shard_map/all_to_all | solution.py:137
  40.5 0.5 fusion.80
  42.2 0.5 fusion.20
  42.9 0.6 multiply_reduce_fusion
  43.7 0.6 fusion.46
  44.2 0.6 fusion.53
  44.9 0.6 convolution_subtract_fusion.2
  45.5 0.6 convolution_add_fusion.2
  46.0 0.5 fusion.77
  47.7 0.5 fusion.27
  48.9 3.8 %all_to_all.61 = bf16[2,2,13824]{2,1,0:T(2,128)(2,1)S(1)} all-to-all(bf16[2,2,13824]{2,1,0:T(2,128)(2,1)S(1)} %reshape.449), channel_id=1, replica_groups=mesh['node'=8,'span_0'=4,'span_1'=12,'span_2'=2] {'span_2'}, dimensions={0} | all-to-all | bytes 221184 | tf_op jit(solution)/shard_map/all_to_all | solution.py:28
  53.3 1.1 reshape.451
  54.4 4.9 %all-to-all-start.2 = ((bf16[48,2,576]{2,1,0:T(2,128)(2,1)}), bf16[48,2,576]{2,1,0:T(2,128)(2,1)S(1)}, u32[]{:S(2)}, u32[]{:S(2)}) async-start(bf16[48,2,576]{2,1,0:T(2,128)(2,1)} %reshape.451), calls=%async_computation.2 | async-start | bytes 245760 | tf_op jit(solution)/shard_map/all_to_all | solution.py:28
  59.3 0.8 add_multiply_fusion
  60.1 1.9 %fusion.6 = f32[2,2,576,48]{2,3,1,0:T(8,128)S(1)} fusion(f32[576,576]{1,0:T(8,128)S(1)} %copy-done, f32[1,2,576,48]{2,3,1,0:T(8,128)S(1)} %copy-done.2, f32[1,2,576,48]{2,3,1,0:T(8,128)S(1)} %bitcast.156), kind=kOutput, calls=%fused_computation.6 | convolution fusion | flops 764522496 | bytes 2211840 | tf_op jit(solution)/shard_map/yx,mcxq->mcyq/dot_general | solution.py:117
  62.0 11.1 %all-to-all-done.2 = bf16[48,2,576]{2,1,0:T(2,128)(2,1)S(1)} async-done(((bf16[48,2,576]{2,1,0:T(2,128)(2,1)}), bf16[48,2,576]{2,1,0:T(2,128)(2,1)S(1)}, u32[]{:S(2)}, u32[]{:S(2)}) %all-to-all-start.2) | async-done | bytes 110624 | tf_op jit(solution)/shard_map/all_to_all | solution.py:28
  74.1 1.0 fusion.21
  75.2 18.9 %all_to_all.62 = f32[1,2,576,48]{2,1,0,3:T(2,128)S(1)} all-to-all(f32[1,2,576,48]{2,1,0,3:T(2,128)S(1)} %copy.93), channel_id=1, replica_groups=mesh['node'=8,'span_0'=4,'span_1'=12,'span_2'=2] {'node'}, dimensions={3} | all-to-all | bytes 442368 | tf_op jit(solution)/shard_map/all_to_all | solution.py:150
  94.6 14.5 %all_to_all.63 = f32[8,2,576,6]{2,1,3,0:T(2,128)S(1)} all-to-all(f32[8,2,576,6]{2,1,3,0:T(2,128)S(1)} %copy.95), channel_id=1, replica_groups=mesh['node'=8,'span_0'=4,'span_1'=12,'span_2'=2] {'node'}, dimensions={0} | all-to-all | bytes 442368 | tf_op jit(solution)/shard_map/all_to_all | solution.py:152
  109.1 2.2 %fusion.12 = f32[1,2,576,48]{2,3,1,0:T(8,128)} fusion(f32[576,576]{1,0:T(8,128)S(1)} %copy-done.1, f32[2,2,576,48]{2,3,1,0:T(8,128)S(1)} %fusion.6, f32[1,2,576,48]{2,1,3,0:T(2,128)S(1)} %bitcast.154, f32[576,48]{0,1:T(8,128)S(1)} %get-tuple-element.13, f32[576,48]{0,1:T(8,128)S(1)} %get-tuple-element.11), kind=kOutput, calls=%fused_computation.8 | convolution fusion | flops 382427136 | bytes 2433024 | tf_op jit(solution)/shard_map/yx,mcxq->mcyq/dot_general | solution.py:117
  (53 shorter events, 9.3 us)
Async XLA Ops:
  0.0 60.1 %copy-start = (f32[576,576]{1,0:T(8,128)S(1)}, f32[576,576]{1,0:T(8,128)}, u32[]{:S(2)}) copy-start(f32[576,576]{1,0:T(8,128)} %param.12) | copy-start | bytes 3981316
  0.0 22.1 %copy-start.7 = (f32[8]{0:T(128)S(1)}, f32[8]{0:T(128)}, u32[]{:S(2)}) copy-start(f32[8]{0:T(128)} %constant.101.clone) | copy-start | bytes 100
  2.5 34.7 %all-to-all-start = ((bf16[96,2,288]{2,1,0:T(2,128)(2,1)}), bf16[96,2,288]{2,1,0:T(2,128)(2,1)S(1)}, u32[]{:S(2)}, u32[]{:S(2)}) async-start(bf16[96,2,288]{2,1,0:T(2,128)(2,1)} %reshape.447), calls=%async_computation | async-start | bytes 294912 | tf_op jit(solution)/shard_map/all_to_all | solution.py:137
  41.0 2.0 %copy-start.4 = (f32[1,6,4608]{2,0,1:T(1,128)S(1)}, f32[1,6,4608]{2,0,1:T(1,128)}, u32[]{:S(2)}) copy-start(f32[1,6,4608]{2,0,1:T(1,128)} %param.10) | copy-start | bytes 331780
  48.4 10.9 %copy-start.5 = (f32[576]{0:T(1024)S(1)}, f32[576]{0:T(1024)}, u32[]{:S(2)}) copy-start(f32[576]{0:T(1024)} %param.13) | copy-start | bytes 6916
  48.5 11.7 %copy-start.2 = (f32[1,2,576,48]{2,3,1,0:T(8,128)S(1)}, f32[1,2,576,48]{2,3,1,0:T(8,128)}, u32[]{:S(2)}) copy-start(f32[1,2,576,48]{2,3,1,0:T(8,128)} %param.8) | copy-start | bytes 663556
  48.5 11.6 %copy-start.3 = (f32[2,576,48]{1,2,0:T(8,128)S(1)}, f32[2,576,48]{1,2,0:T(8,128)}, u32[]{:S(2)}) copy-start(f32[2,576,48]{1,2,0:T(8,128)} %param.9) | copy-start | bytes 663556
  54.4 18.7 %all-to-all-start.2 = ((bf16[48,2,576]{2,1,0:T(2,128)(2,1)}), bf16[48,2,576]{2,1,0:T(2,128)(2,1)S(1)}, u32[]{:S(2)}, u32[]{:S(2)}) async-start(bf16[48,2,576]{2,1,0:T(2,128)(2,1)} %reshape.451), calls=%async_computation.2 | async-start | bytes 245760 | tf_op jit(solution)/shard_map/all_to_all | solution.py:28
  74.0 20.0 %copy-start.6 = (f32[8,8,1,1]{1,0,3,2:T(8,128)S(1)}, f32[8,8,1,1]{1,0,3,2:T(8,128)}, u32[]{:S(2)}) copy-start(f32[8,8,1,1]{1,0,3,2:T(8,128)} %constant.105) | copy-start | bytes 772
  75.0 34.1 %copy-start.1 = (f32[576,576]{1,0:T(8,128)S(1)}, f32[576,576]{1,0:T(8,128)}, u32[]{:S(2)}) copy-start(f32[576,576]{1,0:T(8,128)} %param.11) | copy-start | bytes 3981316
where the time goes:
time: 112 us; the launch traced here: 111 us
  blocking collectives  37.2 us (33%)
  waiting for transfers between devices  25.2 us (22%)
  starting transfers between devices  24.5 us (22%)
  matrix products  13.2 us (12%)
  local copies, waits for them, and re-layouts  7.81 us (7%)
  other arithmetic  2.97 us (3%)
    all_to_all x1, starting transfers between devices, local(): lax.all_to_all(gradient, SPAN, split_axis=2, concat_axis=3, tiled=True)  19.6 us
    all_to_all x1, blocking collectives, local(): lax.all_to_all(section_term, 'node', split_axis=3, concat_axis=0, tiled=T...  18.9 us
    all_to_all x1, blocking collectives, local(): lax.all_to_all(blended, 'node', split_axis=0, concat_axis=3, tiled=True)[0]  14.5 us
    all_to_all x1, waiting for transfers between devices, local(): lax.all_to_all(gradient, SPAN, split_axis=2, concat_axis=3, tiled=True)  14.1 us
    all_to_all x1, waiting for transfers between devices, turned_blocks(): out = lax.all_to_all(out, axes[k], k, k, tiled=True)  11.1 us
    dot_general x3, matrix products, eigen_apply(): jnp.einsum('yx,mcxq->mcyq', matrix, fields, precision=lax.Precision.HIGHEST)  5.08 us
    all_to_all x1, starting transfers between devices, turned_blocks(): out = lax.all_to_all(out, axes[k], k, k, tiled=True)  4.89 us
    all_to_all x1, blocking collectives, turned_blocks(): out = lax.all_to_all(out, axes[k], k, k, tiled=True)  3.81 us
  transfers between devices with their start and end apart: 2, of which 2 were waited for; matrix products, arithmetic and copies ran while one was open for 3% of the time, Pallas kernels for 0%

commit v1 on v0

v1 whole, which is shorter than its diff:
```python
import functools
import math

import jax
import jax.numpy as jnp
import ml_dtypes
import numpy as np
from jax import lax
from jax.experimental import pallas as pl
from jax.experimental.pallas import tpu as pltpu
from jax.sharding import PartitionSpec as P

MESH = pl.DeviceIdType.MESH
BF = jnp.bfloat16
F32 = jnp.float32
HALF = 64
LANES = 128


def collocation(node_total):
    points = [
        0.5 - 0.5 * math.cos((2.0 * m + 1.0) * math.pi / (2.0 * node_total))
        for m in range(node_total)
    ]
    weights = [[0.0] * node_total for _ in range(node_total)]
    for column in range(node_total):
        coeffs = [1.0]
        scale = 1.0
        for other in range(node_total):
            if other != column:
                grown = [0.0] * (len(coeffs) + 1)
                for power in range(len(coeffs)):
                    grown[power + 1] += coeffs[power]
                    grown[power] -= points[other] * coeffs[power]
                coeffs = grown
                scale = scale * (points[column] - points[other])
        for row in range(node_total):
            total = 0.0
            for power in range(len(coeffs)):
                total += coeffs[power] * points[row] ** (power + 1) / (power + 1)
            weights[row][column] = total / scale
    return (weights, [value / node_total for value in points])


def split_np(table):
    high = table.astype(np.float32).astype(ml_dtypes.bfloat16)
    low = (table - high.astype(np.float64)).astype(ml_dtypes.bfloat16)
    return high, low


def tables(span, local_modes, lines):
    nz = span * local_modes
    s = np.arange(span, dtype=np.int64)
    r = np.arange(local_modes, dtype=np.int64)
    outer = 2 * np.pi * ((s[:, None] * s[None, :]) % span) / span
    inner = 2 * np.pi * ((r[:, None] * r[None, :]) % local_modes) / local_modes
    twist = 2 * np.pi * (s[:, None] * r[None, :]) / nz
    first = np.zeros((LANES, 2 * span))
    first[:span, :span] = np.cos(outer)
    first[:span, span:] = np.sin(outer)
    last = np.zeros((LANES, 2 * LANES))
    last[:span, :span] = np.cos(outer)
    last[:span, LANES : LANES + span] = np.sin(outer)

    def complex_block(phase):
        block = np.zeros((LANES, LANES))
        n = local_modes
        block[:n, :n] = np.cos(phase)
        block[:n, HALF : HALF + n] = -np.sin(phase)
        block[HALF : HALF + n, :n] = np.sin(phase)
        block[HALF : HALF + n, HALF : HALF + n] = np.cos(phase)
        return block

    to_points = complex_block(inner)
    to_modes = complex_block(-inner)
    cosine, sine = np.zeros((LANES, LANES)), np.zeros((LANES, LANES))
    cosine[:span, :local_modes] = np.cos(twist)
    cosine[:span, HALF : HALF + local_modes] = np.cos(twist)
    sine[:span, :local_modes] = -np.sin(twist)
    sine[:span, HALF : HALF + local_modes] = np.sin(twist)
    turns = np.concatenate([cosine, sine, cosine.T, -sine.T], axis=1).astype(np.float32)
    group = math.gcd(16, span)
    spread = np.zeros((LANES, 2 * LANES))
    for g in range(group):
        for y in range(lines):
            spread[g * 8 + y, g * lines + y] = 1.0
            spread[g * lines + y, LANES + g * 8 + y] = 1.0
    width = 2 * LANES

    def wide(a):
        out = np.zeros((LANES, width), ml_dtypes.bfloat16)
        out[:, : a.shape[1]] = a
        return out

    parts = []
    for table in (first, last):
        parts += [wide(t) for t in split_np(table)]
    for table in (to_points, to_modes):
        parts.append(np.concatenate(split_np(table), axis=1))
    parts.append(wide(spread.astype(ml_dtypes.bfloat16)))
    return np.concatenate(parts, axis=0), turns


def dot(a, b):
    return jnp.dot(a, b, preferred_element_type=F32)


def dot_t(a, b):
    return lax.dot_general(a, b, (((1,), (1,)), ((), ())), preferred_element_type=F32)


def split(x):
    high = x.astype(BF)
    return high, (x - high.astype(F32)).astype(BF)


def three(product, a, b):
    return product(a[0], b[0]) + (product(a[0], b[1]) + product(a[1], b[0]))


def side_by_side(pair_ref, local_modes):
    rows = pair_ref.shape[1]
    gap = jnp.zeros((rows, HALF - local_modes), F32)
    return jnp.concatenate([pair_ref[0], gap, pair_ref[1], gap], axis=1)


def turned(x):
    return pltpu.roll(x, HALF, axis=1)


def sweep(
    nodes, span, lines, quadrature, shifts,
    it_ref, st_ref, vel_ref, eig_ref, inv_ref, rate_ref, mats_ref, turns_ref,
    out_ref,
    fields, inv_hi, inv_lo, eig_hi, eig_lo, velocity, coeff, base, inverse_den,
    lines_f32, e1_out, e1_in, r_in, r_out, r_all, e2_out, e2_in, a_out, a_all,
    e1_send, e1_recv, rt_send, rt_recv, rb_send, rb_recv,
    e2_send, e2_own, e2_recv, ab_send, ab_recv,
):
    ny, local_modes = it_ref.shape[1], it_ref.shape[2]
    share = span // nodes
    rows = ny // nodes
    node, me = lax.axis_index("node"), lax.axis_index("span")
    nz = span * local_modes

    barrier = pltpu.get_barrier_semaphore()

    def greet(k, carry):
        pl.semaphore_signal(
            barrier, 1, device_id={"span": lax.rem(me + k, span)}, device_id_type=MESH
        )
        return carry

    lax.fori_loop(1, span, greet, 0)
    for k in range(1, nodes):
        pl.semaphore_signal(
            barrier, 1, device_id={"node": lax.rem(node + k, nodes)}, device_id_type=MESH
        )

    lane = lax.broadcasted_iota(jnp.int32, (1, LANES), 1)
    mode = me * local_modes + lax.rem(lane, HALF)
    signed = jnp.where(mode < nz // 2, mode, mode - nz).astype(F32) / (nz // 2)
    turn_sign = jnp.where(lane < HALF, -1.0, 1.0).astype(F32)
    fields[...] = side_by_side(it_ref, local_modes)
    gradient = (turned(fields[...]) * (signed * turn_sign)).astype(BF)
    group = math.gcd(16, span)
    spread = mats_ref[pl.ds(6 * LANES, group * 8), : group * lines]
    gather = mats_ref[pl.ds(6 * LANES, group * lines), LANES : LANES + group * 8]
    for g in range(span // group):
        block = dot(spread, gradient[g * group * lines : (g + 1) * group * lines])
        e1_out[pl.ds(g * group, group)] = block.reshape(group, 8, LANES).astype(BF)
    high, low = split(inv_ref[...])
    inv_hi[...] = high
    inv_lo[...] = low
    high, low = split(eig_ref[...])
    eig_hi[...] = high
    eig_lo[...] = low
    inverse = (inv_hi, inv_lo)

    def by_inverse(x):
        return three(dot, (inv_hi[...], inv_lo[...]), split(x))

    start = side_by_side(st_ref, local_modes)
    coeff[...] = by_inverse(jnp.concatenate([fields[...], start], axis=1))
    velocity[...] = jnp.zeros_like(velocity)
    for y in range(lines):
        part = vel_ref[y] * (-1.0 / nz)
        velocity[0:local_modes, y * LANES : y * LANES + span] = part
        velocity[HALF : HALF + local_modes, y * LANES : y * LANES + span] = part
    lines_f32[...] = jnp.zeros_like(lines_f32)

    pl.semaphore_wait(barrier, span - 1 + nodes - 1)

    def send_lines(k, carry):
        peer = lax.rem(me + k, span)
        pltpu.make_async_remote_copy(
            src_ref=e1_out.at[peer], dst_ref=e1_in.at[me], send_sem=e1_send, recv_sem=e1_recv,
            device_id={"span": peer}, device_id_type=MESH,
        ).start()
        return carry

    lax.fori_loop(1, span, send_lines, 0)

    def node_copies(source, target, send_sem, recv_sem):
        out = []
        for k in range(1, nodes):
            peer = lax.rem(node + k, nodes)
            out.append(
                pltpu.make_async_remote_copy(
                    src_ref=source(peer), dst_ref=target, send_sem=send_sem, recv_sem=recv_sem,
                    device_id={"node": peer}, device_id_type=MESH,
                )
            )
        for copy in out:
            copy.start()

    node_copies(
        lambda peer: fields.at[pl.ds(pl.multiple_of(peer * rows, 8), rows)],
        r_in.at[node], rt_send, rt_recv,
    )
    e1_in[me] = e1_out[me]
    r_in[node] = fields[pl.ds(pl.multiple_of(node * rows, 8), rows)]
    some = pl.ds(0, nodes - 1)
    pltpu.make_async_copy(r_in.at[some], r_out.at[some], rt_recv).wait()

    def blend_fields(i, carry):
        at = pl.ds(pl.multiple_of(i * 8, 8), 8)
        terms = [r_in[j, at] for j in range(nodes)]
        for m in range(nodes):
            total = terms[0] * quadrature[m][0]
            for j in range(1, nodes):
                total = total + terms[j] * quadrature[m][j]
            r_out[m, at] = total
        return carry

    lax.fori_loop(0, rows // 8, blend_fields, 0)
    node_copies(lambda peer: r_out.at[peer], r_all.at[node], rb_send, rb_recv)
    r_all[node] = r_out[node]

    most = pl.ds(0, span - 1)
    pltpu.make_async_copy(e1_out.at[most], e1_in.at[most], e1_recv).wait()

    lines_f32[...] = e1_in[...].astype(F32)
    columns = [lines_f32[:, y, :] for y in range(lines)]
    stacked = jnp.concatenate(
        [
            jnp.concatenate(columns, axis=1),
            jnp.concatenate([turned(c) * turn_sign for c in columns], axis=1),
        ],
        axis=0,
    ).astype(BF)
    two = pl.ds(0, LANES)
    first_hi = mats_ref[pl.ds(0, LANES), : 2 * span]
    first_lo = mats_ref[pl.ds(LANES, LANES), : 2 * span]
    grid = dot(first_hi, stacked) + dot(first_lo, stacked)
    cosine, sine = turns_ref[:, 0:LANES], turns_ref[:, LANES : 2 * LANES]
    pieces = []
    for y in range(lines):
        piece = grid[:, y * LANES : (y + 1) * LANES]
        pieces.append(piece * cosine + turned(piece) * sine)
    tall = split(jnp.concatenate(pieces, axis=0))
    to_points = [mats_ref[pl.ds(4 * LANES, LANES), i * LANES : (i + 1) * LANES] for i in (0, 1)]
    to_modes = [mats_ref[pl.ds(5 * LANES, LANES), i * LANES : (i + 1) * LANES] for i in (0, 1)]
    physical = three(dot_t, to_points, tall)
    modes = three(dot, to_modes, split(physical * velocity[...]))
    swapped = jnp.concatenate([modes[HALF:], modes[:HALF]], axis=0)
    cosine, sine = turns_ref[:, 2 * LANES : 3 * LANES], turns_ref[:, 3 * LANES : 4 * LANES]
    pieces = []
    for y in range(lines):
        at = slice(y * LANES, (y + 1) * LANES)
        piece = modes[:, at] * cosine + swapped[:, at] * sine
        other = jnp.concatenate([piece[HALF:], -piece[:HALF]], axis=0)
        pieces.append(jnp.concatenate([piece, other], axis=1))
    tall = split(jnp.concatenate(pieces, axis=0))
    last = [mats_ref[pl.ds(i * LANES, span), :] for i in (2, 3)]
    spectral = three(dot_t, last, tall)
    for y in range(lines):
        lines_f32[:, y, :] = spectral[:, y * LANES : (y + 1) * LANES]
    e2_out[...] = lines_f32[...].astype(BF)

    combiner = me // share
    slot = node * share + lax.rem(me, share)

    def send_modes(k, carry):
        peer = lax.rem(me + k, span)
        pltpu.make_async_remote_copy(
            src_ref=e2_out.at[peer], dst_ref=e2_in.at[slot], send_sem=e2_send, recv_sem=e2_recv,
            device_id={"node": combiner, "span": peer}, device_id_type=MESH,
        ).start()
        return carry

    lax.fori_loop(1, span, send_modes, 0)
    own = pltpu.make_async_remote_copy(
        src_ref=e2_out.at[me], dst_ref=e2_in.at[slot], send_sem=e2_own, recv_sem=e2_recv,
        device_id={"node": combiner}, device_id_type=MESH,
    )

    @pl.when(combiner != node)
    def _():
        own.start()

    @pl.when(combiner == node)
    def _():
        pltpu.make_async_copy(e2_out.at[me], e2_in.at[slot], e2_recv).start()

    pltpu.make_async_copy(r_out.at[some], r_all.at[some], rb_recv).wait()
    shift = jnp.float32(0.0)
    for m in range(nodes):
        shift = jnp.where(node == m, jnp.float32(shifts[m]), shift)
    damping = rate_ref[...] + signed * signed
    weighted = by_inverse(r_all[...].reshape(ny, LANES))
    inverse_den[...] = 1.0 / (1.0 + shift * damping)
    known = coeff[:, LANES:] - damping * weighted + (shift * damping) * coeff[:, :LANES]
    base[...] = three(
        dot, (eig_hi[...], eig_lo[...]), split(known * inverse_den[...])
    )

    pltpu.make_async_copy(e2_out, e2_in, e2_recv).wait()

    def blend_modes(i, carry):
        terms = [e2_in[j * share + i].astype(F32) for j in range(nodes)]
        for m in range(nodes):
            total = terms[0] * quadrature[m][0]
            for j in range(1, nodes):
                total = total + terms[j] * quadrature[m][j]
            a_out[m, i] = total.astype(BF)
        return carry

    lax.fori_loop(0, share, blend_modes, 0)
    node_copies(lambda peer: a_out.at[peer], a_all.at[node], ab_send, ab_recv)
    a_all[node] = a_out[node]
    pltpu.make_async_copy(a_out.at[some], a_all.at[some], ab_recv).wait()
    arrived = a_all[...].astype(F32).reshape(span * 8, LANES).astype(BF)
    terms = []
    for g in range(span // group):
        terms.append(dot(gather, arrived[g * group * 8 : (g + 1) * group * 8]))
    term = jnp.concatenate(terms, axis=0).astype(BF)
    projected = dot(inv_hi[...], term) + dot(inv_lo[...], term)
    result = base[...] + three(
        dot, (eig_hi[...], eig_lo[...]), split(projected * inverse_den[...])
    )
    out_ref[0] = result[:, :local_modes]
    out_ref[1] = result[:, HALF : HALF + local_modes]

    pltpu.make_async_copy(e1_out.at[most], e1_in.at[most], e1_send).wait()
    pltpu.make_async_copy(r_in.at[some], r_out.at[some], rt_send).wait()
    pltpu.make_async_copy(r_out.at[some], r_all.at[some], rb_send).wait()
    pltpu.make_async_copy(e2_out.at[most], e2_in.at[most], e2_send).wait()
    pltpu.make_async_copy(a_out.at[some], a_all.at[some], ab_send).wait()

    @pl.when(combiner != node)
    def _():
        own.wait_send()


def local(nodes, span, iterate, start_field, spanwise_velocity, eigen_basis, inverse_basis, decay_rates):
    ny, local_modes = iterate.shape[2], iterate.shape[3]
    lines = spanwise_velocity.shape[1]
    share, rows = span // nodes, ny // nodes
    quadrature, shifts = collocation(nodes)
    mats, turns = tables(span, local_modes, lines)
    velocity = spanwise_velocity[0].reshape(lines, local_modes, span)
    vmem = pl.BlockSpec(memory_space=pltpu.VMEM)
    sem = pltpu.SemaphoreType.DMA
    return pl.pallas_call(
        functools.partial(sweep, nodes, span, lines, quadrature, shifts),
        out_shape=jax.ShapeDtypeStruct((2, ny, local_modes), F32),
        in_specs=[vmem] * 8,
        out_specs=vmem,
        scratch_shapes=[
            pltpu.VMEM((ny, LANES), F32),
            pltpu.VMEM((ny, ny), BF),
            pltpu.VMEM((ny, ny), BF),
            pltpu.VMEM((ny, ny), BF),
            pltpu.VMEM((ny, ny), BF),
            pltpu.VMEM((LANES, lines * LANES), F32),
            pltpu.VMEM((ny, 2 * LANES), F32),
            pltpu.VMEM((ny, LANES), F32),
            pltpu.VMEM((ny, LANES), F32),
            pltpu.VMEM((span, 8, LANES), F32),
            pltpu.VMEM((span, 8, LANES), BF),
            pltpu.VMEM((span, 8, LANES), BF),
            pltpu.VMEM((nodes, rows, LANES), F32),
            pltpu.VMEM((nodes, rows, LANES), F32),
            pltpu.VMEM((nodes, rows, LANES), F32),
            pltpu.VMEM((span, 8, LANES), BF),
            pltpu.VMEM((span, 8, LANES), BF),
            pltpu.VMEM((nodes, share, 8, LANES), BF),
            pltpu.VMEM((nodes, share, 8, LANES), BF),
        ]
        + [sem] * 11,
        compiler_params=pltpu.CompilerParams(
            collective_id=0, has_side_effects=True, vmem_limit_bytes=40 << 20
        ),
    )(
        iterate[0], start_field, velocity, eigen_basis, inverse_basis,
        decay_rates[:, None], jnp.asarray(mats), jnp.asarray(turns),
    )[None]


def solution(mesh):
    return jax.shard_map(
        functools.partial(local, mesh.shape["node"], mesh.shape["span"]),
        mesh=mesh,
        in_specs=(
            P("node", None, None, "span"),
            P(None, None, "span"),
            P("node", "span", None),
            P(),
            P(),
            P(),
        ),
        out_specs=P("node", None, None, "span"),
        check_vma=False,
    )
```

time: 112 us -> 73.8 us (0.66)
  the two profiles are of different devices: /device:TPU:8 before, /device:TPU:24 now
where the time goes in v1:
time: 73.8 us; the launch traced here: 73.4 us
  Pallas kernels  63 us (85%)
  local copies, waits for them, and re-layouts  9.05 us (12%)
  other arithmetic  1.27 us (2%)
    pallas_call x1, Pallas kernels, local(): pl.pallas_call(functools.partial(sweep, nodes, span, lines, quadrature, s...  63 us
    unnamed x12, local copies, waits for them, and re-layouts  6.57 us

profile of v1, /device:TPU:24, one launch (start us, length us, event | category | flops | bytes accessed | tf_op | source)
XLA Modules:
  0.0 73.4 jit_solution(1138366252710171237)
XLA Ops:
  0.0 0.0 copy-start
  0.0 1.3 %reduce = f32[6,4608]{1,0:T(8,128)S(1)} reduce(f32[1,6,4608]{2,0,1:T(1,128)} %param.10, f32[]{:T(128)} %constant.9), dimensions={0}, to_apply=%param.10.reduce_sub_computation | reduce | bytes 221188 | tf_op args[2]
  1.3 0.8 %reshape_squeeze.3.vel_ref = f32[6,48,96]{2,1,0:T(8,128)} reshape(f32[6,4608]{1,0:T(8,128)S(1)} %reduce) | data formatting | bytes 221184 | tf_op jit(solution)/shard_map/reshape;squeeze | solution.py:362
  2.0 0.8 %broadcast_in_dim.8.rate_ref = f32[576,1]{1,0:T(8,128)S(1)} reshape(f32[576]{0:T(1024)} %param.13) | data formatting | bytes 4608 | tf_op jit(solution)/shard_map/broadcast_in_dim | solution.py:397
  2.9 1.2 %copy.12 = f32[1,2,576,48]{3,2,1,0:T(8,128)S(1)} copy(f32[1,2,576,48]{2,3,1,0:T(8,128)} %param.8) | data formatting | bytes 442368 | tf_op args[0]
  4.0 1.2 %copy.13.st_ref = f32[2,576,48]{2,1,0:T(8,128)S(1)} copy(f32[2,576,48]{1,2,0:T(8,128)} %param.9) | data formatting | bytes 442368 | tf_op args[1]
  5.2 0.0 copy-done
  5.2 0.0 copy-start.1
  5.2 1.4 %copy-done.1 = f32[576,576]{1,0:T(8,128)S(1)} copy-done((f32[576,576]{1,0:T(8,128)S(1)}, f32[576,576]{1,0:T(8,128)}, u32[]{:S(2)}) %copy-start.1) | copy-done | bytes 1327128
  6.6 0.0 copy-start.2
  6.6 0.9 %copy-done.2 = f32[6,48,96]{2,1,0:T(8,128)S(1)} copy-done((f32[6,48,96]{2,1,0:T(8,128)S(1)}, f32[6,48,96]{2,1,0:T(8,128)}, u32[]{:S(2)}) %copy-start.2) | copy-done | bytes 110616
  7.5 0.0 copy-start.3
  7.5 1.0 %copy-done.3 = bf16[896,256]{1,0:T(8,128)(2,1)S(1)} copy-done((bf16[896,256]{1,0:T(8,128)(2,1)S(1)}, bf16[896,256]{1,0:T(8,128)(2,1)}, u32[]{:S(2)}) %copy-start.3) | copy-done | bytes 458776
  8.5 0.0 copy-start.4
  8.5 0.9 %copy-done.4 = f32[128,512]{1,0:T(8,128)S(1)} copy-done((f32[128,512]{1,0:T(8,128)S(1)}, f32[128,512]{1,0:T(8,128)}, u32[]{:S(2)}) %copy-start.4) | copy-done | bytes 262168
  9.5 63.0 %shard_map.82 = f32[2,576,48]{2,1,0:T(8,128)S(1)} custom-call(f32[2,576,48]{2,1,0:T(8,128)S(1)} %bitcast.3, f32[2,576,48]{2,1,0:T(8,128)S(1)} %copy.13.st_ref, f32[6,48,96]{2,1,0:T(8,128)S(1)} %copy-done.2, f32[576,576]{1,0:T(8,128)S(1)} %copy-done, f32[576,576]{1,0:T(8,128)S(1)} %copy-done.1, f32[576,1]{1,0:T(8,128)S(1)} %broadcast_in_dim.8.rate_ref, ...), custom_call_target="tpu_custom_call" | custom-call | tf_op jit(solution)/shard_map/pallas_call | solution.py:365
  72.5 0.9 %copy.15 = f32[1,2,576,48]{2,3,1,0:T(8,128)} copy(f32[1,2,576,48]{3,2,1,0:T(8,128)S(1)} %bitcast.2) | data formatting | bytes 442368 | tf_op jit(solution)/shard_map/broadcast_in_dim | solution.py:365
Async XLA Ops:
  0.0 5.2 %copy-start = (f32[576,576]{1,0:T(8,128)S(1)}, f32[576,576]{1,0:T(8,128)}, u32[]{:S(2)}) copy-start(f32[576,576]{1,0:T(8,128)} %eig_ref.1) | copy-start | bytes 3981316
  5.2 1.4 %copy-start.1 = (f32[576,576]{1,0:T(8,128)S(1)}, f32[576,576]{1,0:T(8,128)}, u32[]{:S(2)}) copy-start(f32[576,576]{1,0:T(8,128)} %inv_ref.1) | copy-start | bytes 3981316
  6.6 0.9 %copy-start.2 = (f32[6,48,96]{2,1,0:T(8,128)S(1)}, f32[6,48,96]{2,1,0:T(8,128)}, u32[]{:S(2)}) copy-start(f32[6,48,96]{2,1,0:T(8,128)} %reshape_squeeze.3.vel_ref) | copy-start | bytes 331780
  7.5 1.0 %copy-start.3 = (bf16[896,256]{1,0:T(8,128)(2,1)S(1)}, bf16[896,256]{1,0:T(8,128)(2,1)}, u32[]{:S(2)}) copy-start(bf16[896,256]{1,0:T(8,128)(2,1)} %constant.4.clone.mats_ref) | copy-start | bytes 1376260
  8.5 0.9 %copy-start.4 = (f32[128,512]{1,0:T(8,128)S(1)}, f32[128,512]{1,0:T(8,128)}, u32[]{:S(2)}) copy-start(f32[128,512]{1,0:T(8,128)} %constant.5.clone.turns_ref) | copy-start | bytes 786436

commit v2 on v1

v2 whole, which is shorter than its diff:
```python
import functools
import math
from types import SimpleNamespace

import jax
import jax.numpy as jnp
import ml_dtypes
import numpy as np
from jax import lax
from jax.experimental import pallas as pl
from jax.experimental.pallas import tpu as pltpu
from jax.sharding import PartitionSpec as P

MESH = pl.DeviceIdType.MESH
BF = jnp.bfloat16
F32 = jnp.float32
HALF = 64
LANES = 128


def collocation(node_total):
    points = [
        0.5 - 0.5 * math.cos((2.0 * m + 1.0) * math.pi / (2.0 * node_total))
        for m in range(node_total)
    ]
    weights = [[0.0] * node_total for _ in range(node_total)]
    for column in range(node_total):
        coeffs = [1.0]
        scale = 1.0
        for other in range(node_total):
            if other != column:
                grown = [0.0] * (len(coeffs) + 1)
                for power in range(len(coeffs)):
                    grown[power + 1] += coeffs[power]
                    grown[power] -= points[other] * coeffs[power]
                coeffs = grown
                scale = scale * (points[column] - points[other])
        for row in range(node_total):
            total = 0.0
            for power in range(len(coeffs)):
                total += coeffs[power] * points[row] ** (power + 1) / (power + 1)
            weights[row][column] = total / scale
    return (weights, [value / node_total for value in points])


def split_np(table):
    high = table.astype(np.float32).astype(ml_dtypes.bfloat16)
    low = (table - high.astype(np.float64)).astype(ml_dtypes.bfloat16)
    return high, low


def tables(span, local_modes, lines):
    nz = span * local_modes
    s = np.arange(span, dtype=np.int64)
    r = np.arange(local_modes, dtype=np.int64)
    outer = 2 * np.pi * ((s[:, None] * s[None, :]) % span) / span
    inner = 2 * np.pi * ((r[:, None] * r[None, :]) % local_modes) / local_modes
    twist = 2 * np.pi * (s[:, None] * r[None, :]) / nz
    first = np.zeros((LANES, 2 * span))
    first[:span, :span] = np.cos(outer)
    first[:span, span:] = np.sin(outer)
    last = np.zeros((LANES, 2 * LANES))
    last[:span, :span] = np.cos(outer)
    last[:span, LANES : LANES + span] = np.sin(outer)

    place = (r % 4) * (HALF // 4) + r // 4

    def complex_block(phase, rows, columns):
        block = np.zeros((LANES, LANES))
        for i, row_half in enumerate((0, HALF)):
            for j, column_half in enumerate((0, HALF)):
                value = np.cos(phase) if i == j else (np.sin(phase) if i else -np.sin(phase))
                block[np.ix_(rows + row_half, columns + column_half)] = value
        return block

    to_points = complex_block(inner.T, place, r)
    to_modes = complex_block(-inner, r, place)
    cosine, sine = np.zeros((LANES, LANES)), np.zeros((LANES, LANES))
    cosine[:span, :local_modes] = np.cos(twist)
    cosine[:span, HALF : HALF + local_modes] = np.cos(twist)
    sine[:span, :local_modes] = -np.sin(twist)
    sine[:span, HALF : HALF + local_modes] = np.sin(twist)
    turns = np.concatenate([cosine, sine, cosine.T, -sine.T], axis=1).astype(np.float32)
    group = math.gcd(16, span)
    spread = np.zeros((LANES, 2 * LANES))
    for g in range(group):
        for y in range(lines):
            spread[g * 8 + y, g * lines + y] = 1.0
            spread[g * lines + y, LANES + g * 8 + y] = 1.0
    width = 2 * LANES

    def wide(a):
        out = np.zeros((LANES, width), ml_dtypes.bfloat16)
        out[:, : a.shape[1]] = a
        return out

    parts = []
    for table in (first, last):
        parts += [wide(t) for t in split_np(table)]
    for table in (to_points, to_modes):
        parts.append(np.concatenate(split_np(table), axis=1))
    parts.append(wide(spread.astype(ml_dtypes.bfloat16)))
    return np.concatenate(parts, axis=0), turns


def dot(a, b):
    return jnp.dot(a, b, preferred_element_type=F32)


def dot_t(a, b):
    return lax.dot_general(a, b, (((1,), (1,)), ((), ())), preferred_element_type=F32)


def split(x):
    high = x.astype(BF)
    return high, (x - high.astype(F32)).astype(BF)


def three(product, a, b):
    return product(a[0], b[0]) + (product(a[0], b[1]) + product(a[1], b[0]))


def turned(x):
    return pltpu.roll(x, HALF, axis=1)


def greet(barrier, where):
    pl.semaphore_signal(barrier, 1, device_id=where, device_id_type=MESH)


def greeted(barrier, count):
    pl.semaphore_wait(barrier, count)


def remote(source, target, send_sem, recv_sem, where):
    return pltpu.make_async_remote_copy(
        src_ref=source, dst_ref=target, send_sem=send_sem, recv_sem=recv_sem,
        device_id=where, device_id_type=MESH,
    )


def start(copy):
    copy.start()


def settle(source, target, sem):
    pltpu.make_async_copy(source, target, sem).wait()


def prepare_lines(c, v):
    v.fields_t[...] = jnp.zeros_like(v.fields_t)
    v.fields_t[0 : c.modes] = v.iterate[0]
    v.fields_t[HALF : HALF + c.modes] = v.iterate[1]
    v.fields[...] = v.fields_t[...].T
    gradient = (turned(v.fields[...]) * (c.signed * c.turn_sign)).astype(BF)
    spread = v.mats[pl.ds(6 * LANES, c.group * 8), : c.group * c.lines]
    for g in range(c.span // c.group):
        step = c.group * c.lines
        block = dot(spread, gradient[g * step : (g + 1) * step])
        v.e1_out[pl.ds(g * c.group, c.group)] = block.reshape(c.group, 8, LANES).astype(BF)


def prepare_rest(c, v):
    v.fields_t[0 : c.modes] = v.start_field[0]
    v.fields_t[HALF : HALF + c.modes] = v.start_field[1]
    high, low = split(v.inv[...])
    v.inv_hi[...] = high
    v.inv_lo[...] = low
    high, low = split(v.eig[...])
    v.eig_hi[...] = high
    v.eig_lo[...] = low
    both = jnp.concatenate([v.fields[...], v.fields_t[...].T], axis=1)
    v.coeff[...] = three(dot, (v.inv_hi[...], v.inv_lo[...]), split(both))
    v.damping[...] = jnp.broadcast_to(v.rate[...], (LANES, c.ny)).T + c.signed * c.signed
    v.velocity[...] = jnp.zeros_like(v.velocity)
    for y in range(c.lines):
        for k, part in enumerate(velocity_rows(c, v, y)):
            part = part * (-1.0 / c.nz)
            for half in (0, HALF):
                at = half + k * c.chunk_rows
                v.velocity[at : at + part.shape[0], y * LANES : (y + 1) * LANES] = part
    v.lines_f32[...] = jnp.zeros_like(v.lines_f32)


def velocity_rows(c, v, y):
    count = c.modes // 4
    rows = [v.velocity_in[pl.ds(y * count * 3 + i, count, stride=3), :] for i in range(3)]
    lane = lax.broadcasted_iota(jnp.int32, (1, LANES), 1)

    def rolled(i, by):
        return pltpu.roll(rows[i], by, axis=1)

    return (
        rows[0],
        jnp.where(lane < 32, rolled(0, 32), rolled(1, 32)),
        jnp.where(lane < 64, rolled(1, 64), rolled(2, 64)),
        rolled(2, 96),
    )


def mix(c, terms, m):
    total = terms[0] * c.quadrature[m][0]
    for j in range(1, c.nodes):
        total = total + terms[j] * c.quadrature[m][j]
    return total


def blend_fields(c, v):
    def step(i, carry):
        at = pl.ds(pl.multiple_of(i * 8, 8), 8)
        terms = [v.r_in[j, at] for j in range(c.nodes)]
        for m in range(c.nodes):
            v.r_out[m, at] = mix(c, terms, m)
        return carry

    lax.fori_loop(0, c.rows // 8, step, 0)


def blend_modes(c, v):
    def step(i, carry):
        terms = [v.e2_in[j * c.share + i].astype(F32) for j in range(c.nodes)]
        for m in range(c.nodes):
            v.a_out[m, i] = mix(c, terms, m).astype(BF)
        return carry

    lax.fori_loop(0, c.share, step, 0)


def transform(c, v):
    v.lines_f32[...] = v.e1_in[...].astype(F32)
    columns = [v.lines_f32[:, y, :] for y in range(c.lines)]
    stacked = jnp.concatenate(
        [
            jnp.concatenate(columns, axis=1),
            jnp.concatenate([turned(x) * c.turn_sign for x in columns], axis=1),
        ],
        axis=0,
    ).astype(BF)
    first = [v.mats[pl.ds(i * LANES, LANES), : 2 * c.span] for i in (0, 1)]
    grid = dot(first[0], stacked) + dot(first[1], stacked)
    cosine, sine = v.turns[:, 0:LANES], v.turns[:, LANES : 2 * LANES]
    pieces = []
    for y in range(c.lines):
        piece = grid[:, y * LANES : (y + 1) * LANES]
        pieces.append(piece * cosine + turned(piece) * sine)
    tall = split(jnp.concatenate(pieces, axis=0))
    to_points = [v.mats[pl.ds(4 * LANES, LANES), i * LANES : (i + 1) * LANES] for i in (0, 1)]
    to_modes = [v.mats[pl.ds(5 * LANES, LANES), i * LANES : (i + 1) * LANES] for i in (0, 1)]
    physical = three(dot_t, to_points, tall)
    modes = three(dot, to_modes, split(physical * v.velocity[...]))
    swapped = jnp.concatenate([modes[HALF:], modes[:HALF]], axis=0)
    cosine, sine = v.turns[:, 2 * LANES : 3 * LANES], v.turns[:, 3 * LANES : 4 * LANES]
    pieces = []
    for y in range(c.lines):
        at = slice(y * LANES, (y + 1) * LANES)
        piece = modes[:, at] * cosine + swapped[:, at] * sine
        other = jnp.concatenate([piece[HALF:], -piece[:HALF]], axis=0)
        pieces.append(jnp.concatenate([piece, other], axis=1))
    tall = split(jnp.concatenate(pieces, axis=0))
    last = [v.mats[pl.ds(i * LANES, c.span), :] for i in (2, 3)]
    spectral = three(dot_t, last, tall)
    for y in range(c.lines):
        v.lines_f32[:, y, :] = spectral[:, y * LANES : (y + 1) * LANES]
    v.e2_out[...] = v.lines_f32[...].astype(BF)


def known_part(c, v):
    weighted = three(
        dot, (v.inv_hi[...], v.inv_lo[...]), split(v.r_all[...].reshape(c.ny, LANES))
    )
    damping = v.damping[...]
    v.inverse_den[...] = 1.0 / (1.0 + c.shift * damping)
    known = v.coeff[:, LANES:] - damping * weighted + (c.shift * damping) * v.coeff[:, :LANES]
    v.base[...] = three(dot, (v.eig_hi[...], v.eig_lo[...]), split(known * v.inverse_den[...]))


def finish(c, v, out_ref):
    gather = v.mats[pl.ds(6 * LANES, c.group * c.lines), LANES : LANES + c.group * 8]
    arrived = v.a_all[...].astype(F32).reshape(c.span * 8, LANES).astype(BF)
    terms = []
    for g in range(c.span // c.group):
        terms.append(dot(gather, arrived[g * c.group * 8 : (g + 1) * c.group * 8]))
    term = jnp.concatenate(terms, axis=0).astype(BF)
    projected = dot(v.inv_hi[...], term) + dot(v.inv_lo[...], term)
    result = v.base[...] + three(
        dot, (v.eig_hi[...], v.eig_lo[...]), split(projected * v.inverse_den[...])
    )
    result = result.T
    out_ref[0] = result[0 : c.modes]
    out_ref[1] = result[HALF : HALF + c.modes]


INPUTS = ("iterate", "start_field", "velocity_in", "eig", "inv", "rate", "mats", "turns")


def sweep(sizes, names, *refs):
    c = SimpleNamespace(**sizes)
    count = len(INPUTS)
    sources, out_ref = refs[:count], refs[count]
    v = SimpleNamespace(**dict(zip(names, refs[count + 1 :], strict=True)))
    nodes, span = c.nodes, c.span
    node, me = lax.axis_index("node"), lax.axis_index("span")

    barrier = pltpu.get_barrier_semaphore()

    def greet_span(k, carry):
        greet(barrier, {"span": lax.rem(me + k, span)})
        return carry

    lax.fori_loop(1, span, greet_span, 0)
    for k in range(1, nodes):
        greet(barrier, {"node": lax.rem(node + k, nodes)})

    loads = {
        name: pltpu.make_async_copy(source, getattr(v, name), v.load.at[i])
        for i, (name, source) in enumerate(zip(INPUTS, sources, strict=True))
    }
    order = ("iterate", "mats", "inv", "start_field", "eig", "velocity_in", "rate", "turns")
    for name in order:
        loads[name].start()

    lane = lax.broadcasted_iota(jnp.int32, (1, LANES), 1)
    mode = me * c.modes + lax.rem(lane, HALF)
    c.signed = jnp.where(mode < c.nz // 2, mode, mode - c.nz).astype(F32) / (c.nz // 2)
    c.turn_sign = jnp.where(lane < HALF, -1.0, 1.0).astype(F32)
    c.shift = jnp.float32(0.0)
    for m in range(nodes):
        c.shift = jnp.where(node == m, jnp.float32(c.shifts[m]), c.shift)
    for name in order[:2]:
        loads[name].wait()
    prepare_lines(c, v)
    for name in order[2:]:
        loads[name].wait()
    prepare_rest(c, v)
    greeted(barrier, span - 1 + nodes - 1)

    def send_lines(k, carry):
        peer = lax.rem(me + k, span)
        start(remote(v.e1_out.at[peer], v.e1_in.at[me], v.e1_send, v.e1_recv, {"span": peer}))
        return carry

    lax.fori_loop(1, span, send_lines, 0)

    def to_nodes(source, target, send_sem, recv_sem):
        for k in range(1, nodes):
            peer = lax.rem(node + k, nodes)
            start(remote(source(peer), target, send_sem, recv_sem, {"node": peer}))

    def part(owner):
        return pl.ds(pl.multiple_of(owner * c.rows, 8), c.rows)

    to_nodes(lambda peer: v.fields.at[part(peer)], v.r_in.at[node], v.rt_send, v.rt_recv)
    v.e1_in[me] = v.e1_out[me]
    v.r_in[node] = v.fields[part(node)]
    some, most = pl.ds(0, nodes - 1), pl.ds(0, span - 1)
    settle(v.r_in.at[some], v.r_out.at[some], v.rt_recv)
    blend_fields(c, v)
    to_nodes(lambda peer: v.r_out.at[peer], v.r_all.at[node], v.rb_send, v.rb_recv)
    v.r_all[node] = v.r_out[node]

    settle(v.e1_out.at[most], v.e1_in.at[most], v.e1_recv)
    transform(c, v)

    combiner = me // c.share
    slot = node * c.share + lax.rem(me, c.share)

    def send_modes(k, carry):
        peer = lax.rem(me + k, span)
        where = {"node": combiner, "span": peer}
        start(remote(v.e2_out.at[peer], v.e2_in.at[slot], v.e2_send, v.e2_recv, where))
        return carry

    lax.fori_loop(1, span, send_modes, 0)
    own = remote(v.e2_out.at[me], v.e2_in.at[slot], v.e2_own, v.e2_recv, {"node": combiner})

    @pl.when(combiner != node)
    def _():
        start(own)

    @pl.when(combiner == node)
    def _():
        start(pltpu.make_async_copy(v.e2_out.at[me], v.e2_in.at[slot], v.e2_recv))

    settle(v.r_out.at[some], v.r_all.at[some], v.rb_recv)
    known_part(c, v)

    settle(v.e2_out, v.e2_in, v.e2_recv)
    blend_modes(c, v)
    to_nodes(lambda peer: v.a_out.at[peer], v.a_all.at[node], v.ab_send, v.ab_recv)
    v.a_all[node] = v.a_out[node]
    settle(v.a_out.at[some], v.a_all.at[some], v.ab_recv)
    finish(c, v, out_ref)

    settle(v.e1_out.at[most], v.e1_in.at[most], v.e1_send)
    settle(v.r_in.at[some], v.r_out.at[some], v.rt_send)
    settle(v.r_out.at[some], v.r_all.at[some], v.rb_send)
    settle(v.e2_out.at[most], v.e2_in.at[most], v.e2_send)
    settle(v.a_out.at[some], v.a_all.at[some], v.ab_send)

    @pl.when(combiner != node)
    def _():
        settle(v.e2_out.at[0], v.e2_in.at[0], v.e2_own)


def local(nodes, span, iterate, start_field, spanwise_velocity, eigen_basis, inverse_basis, decay_rates):
    ny, modes = iterate.shape[2], iterate.shape[3]
    lines = spanwise_velocity.shape[1]
    share, rows = span // nodes, ny // nodes
    quadrature, shifts = collocation(nodes)
    mats, turns = tables(span, modes, lines)
    operands = [
        jnp.swapaxes(iterate[0], 1, 2),
        jnp.swapaxes(start_field, 1, 2),
        spanwise_velocity.reshape(-1, LANES),
        eigen_basis,
        inverse_basis,
        decay_rates[None],
        jnp.asarray(mats),
        jnp.asarray(turns),
    ]
    sizes = dict(
        nodes=nodes, span=span, lines=lines, modes=modes, ny=ny, nz=span * modes, share=share,
        rows=rows, group=math.gcd(16, span), chunk_rows=HALF // 4,
        quadrature=quadrature, shifts=shifts,
    )
    dma = pltpu.SemaphoreType.DMA
    square = pltpu.VMEM((ny, ny), BF)
    field = pltpu.VMEM((ny, LANES), F32)
    wide = pltpu.VMEM((LANES, lines * LANES), F32)
    lines_bf = pltpu.VMEM((span, 8, LANES), BF)
    parts_f32 = pltpu.VMEM((nodes, rows, LANES), F32)
    parts_bf = pltpu.VMEM((nodes, share, 8, LANES), BF)
    scratch = {name: pltpu.VMEM(x.shape, x.dtype) for name, x in zip(INPUTS, operands, strict=True)}
    scratch |= dict(
        fields_t=pltpu.VMEM((LANES, ny), F32), fields=field, damping=field,
        inv_hi=square, inv_lo=square, eig_hi=square, eig_lo=square,
        velocity=wide, coeff=pltpu.VMEM((ny, 2 * LANES), F32), base=field, inverse_den=field,
        lines_f32=pltpu.VMEM((span, 8, LANES), F32), e1_out=lines_bf, e1_in=lines_bf,
        r_in=parts_f32, r_out=parts_f32, r_all=parts_f32,
        e2_out=lines_bf, e2_in=lines_bf, a_out=parts_bf, a_all=parts_bf,
        load=dma((len(INPUTS),)),
        e1_send=dma, e1_recv=dma, rt_send=dma, rt_recv=dma, rb_send=dma, rb_recv=dma,
        e2_send=dma, e2_own=dma, e2_recv=dma, ab_send=dma, ab_recv=dma,
    )
    updated = pl.pallas_call(
        functools.partial(sweep, sizes, tuple(scratch)),
        out_shape=jax.ShapeDtypeStruct((2, modes, ny), F32),
        in_specs=[pl.BlockSpec(memory_space=pltpu.HBM)] * len(INPUTS),
        out_specs=pl.BlockSpec(memory_space=pltpu.VMEM),
        scratch_shapes=list(scratch.values()),
        compiler_params=pltpu.CompilerParams(
            collective_id=0, has_side_effects=True, vmem_limit_bytes=60 << 20
        ),
    )(*operands)
    return jnp.swapaxes(updated, 1, 2)[None]


def solution(mesh):
    return jax.shard_map(
        functools.partial(local, mesh.shape["node"], mesh.shape["span"]),
        mesh=mesh,
        in_specs=(
            P("node", None, None, "span"),
            P(None, None, "span"),
            P("node", "span", None),
            P(),
            P(),
            P(),
        ),
        out_specs=P("node", None, None, "span"),
        check_vma=False,
    )
```

time: 73.8 us -> 66.2 us (0.90)
  local copies, waits for them, and re-layouts: 9.05 us -> 2.92 us
  other arithmetic: 1.27 us -> 0 us
    unnamed x12 -> x1, local copies, waits for them, and re-layouts: 6.57 us -> 1.65 us
    unnamed x1 -> x0, other arithmetic: 1.27 us -> none
    another operation x1 -> x0, local copies, waits for them, and re-layouts: 0.76 us -> none  [local(): velocity = spanwise_velocity[0].reshape(lines, local_modes, span)]
    broadcast_in_dim x2 -> x1, local copies, waits for them, and re-layouts: 1.72 us -> 1.27 us  [local(): decay_rates[None]]
where the time goes in v2:
time: 66.2 us; the launch traced here: 66 us
  Pallas kernels  63 us (95%)
  local copies, waits for them, and re-layouts  2.92 us (4%)
    pallas_call x1, Pallas kernels, local(): pl.pallas_call(functools.partial(sweep, sizes, tuple(scratch)), out_shape...  63 us
    unnamed x1, local copies, waits for them, and re-layouts  1.65 us

profile of v2, /device:TPU:24, one launch (start us, length us, event | category | flops | bytes accessed | tf_op | source)
XLA Modules:
  0.0 66.0 jit_solution(17374119404592027035)
XLA Ops:
  0.0 1.3 %broadcast_in_dim.6.refs_5_ = f32[1,576]{1,0:T(1,128)} reshape(f32[576]{0:T(1024)} %param.13) | data formatting | bytes 4608 | tf_op jit(solution)/shard_map/broadcast_in_dim | solution.py:417
  1.3 63.0 %shard_map.82 = f32[2,48,576]{2,1,0:T(8,128)} custom-call(f32[2,48,576]{2,1,0:T(8,128)} %bitcast.9, f32[2,48,576]{2,1,0:T(8,128)} %bitcast.10, f32[216,128]{1,0:T(8,128)} %bitcast.11, f32[576,576]{1,0:T(8,128)} %refs_3_.1, f32[576,576]{1,0:T(8,128)} %refs_4_.1, f32[1,576]{1,0:T(1,128)} %broadcast_in_dim.6.refs_5_, bf16[896,256]{1,0:T(8,128)(2,1)} %constant.4.clone.refs_6_, ...), custom_call_target="tpu_custom_call" | custom-call | tf_op jit(solution)/shard_map/pallas_call | solution.py:445
  64.3 1.7 %copy.10 = f32[1,2,576,48]{2,3,1,0:T(8,128)} copy(f32[1,2,576,48]{2,3,1,0:T(8,128)} %bitcast.8) | data formatting | bytes 442368

commit v3 on v2

--- a/solution.py
+++ b/solution.py
@@ -15,6 +15,7 @@
 BF = jnp.bfloat16
 F32 = jnp.float32
 HALF = 64
+RING = 12
 LANES = 128
 
 
@@ -301,13 +302,27 @@
     nodes, span = c.nodes, c.span
     node, me = lax.axis_index("node"), lax.axis_index("span")
 
+    def each_peer(act):
+        chips, runs = c.chips, span // (2 * c.chips)
+        run, chip, core = me // (2 * chips), lax.rem(me // 2, chips), lax.rem(me, 2)
+
+        def ring(chip, others):
+            for d in range(runs - 1, -1, -1):
+                for e in (1, 0):
+                    if others or d or e:
+                        other = lax.rem(run + d, runs) * chips + chip
+                        act(other * 2 + lax.rem(core + e, 2))
+
+        def step(i, carry):
+            away = chips // 2 + ((i + 1) // 2) * (1 - 2 * lax.rem(i, 2))
+            ring(lax.rem(chip + away, chips), True)
+            return carry
+
+        lax.fori_loop(0, chips - 1, step, 0)
+        ring(chip, False)
+
     barrier = pltpu.get_barrier_semaphore()
-
-    def greet_span(k, carry):
-        greet(barrier, {"span": lax.rem(me + k, span)})
-        return carry
-
-    lax.fori_loop(1, span, greet_span, 0)
+    each_peer(lambda peer: greet(barrier, {"span": peer}))
     for k in range(1, nodes):
         greet(barrier, {"node": lax.rem(node + k, nodes)})
 
@@ -333,13 +348,13 @@
         loads[name].wait()
     prepare_rest(c, v)
     greeted(barrier, span - 1 + nodes - 1)
-
-    def send_lines(k, carry):
-        peer = lax.rem(me + k, span)
+    for k in range(1, nodes):
+        greet(v.ready, {"node": lax.rem(node + k, nodes)})
+
+    def send_lines(peer):
         start(remote(v.e1_out.at[peer], v.e1_in.at[me], v.e1_send, v.e1_recv, {"span": peer}))
-        return carry
-
-    lax.fori_loop(1, span, send_lines, 0)
+
+    each_peer(send_lines)
 
     def to_nodes(source, target, send_sem, recv_sem):
         for k in range(1, nodes):
@@ -353,41 +368,40 @@
     v.e1_in[me] = v.e1_out[me]
     v.r_in[node] = v.fields[part(node)]
     some, most = pl.ds(0, nodes - 1), pl.ds(0, span - 1)
+
+    settle(v.e1_out.at[most], v.e1_in.at[most], v.e1_recv)
+    transform(c, v)
+
+    greeted(v.ready, nodes - 1)
+    combiner = me // c.share
+    slot = node * c.share + lax.rem(me, c.share)
+
+    def send_modes(peer):
+        where = {"node": combiner, "span": peer}
+        start(remote(v.e2_out.at[peer], v.e2_in.at[slot], v.e2_send, v.e2_recv, where))
+
+    each_peer(send_modes)
+    own = remote(v.e2_out.at[me], v.e2_in.at[slot], v.e2_own, v.e2_recv, {"node": combiner})
+
+    @pl.when(combiner != node)
+    def _():
+        start(own)
+
+    @pl.when(combiner == node)
+    def _():
+        start(pltpu.make_async_copy(v.e2_out.at[me], v.e2_in.at[slot], v.e2_recv))
+
     settle(v.r_in.at[some], v.r_out.at[some], v.rt_recv)
     blend_fields(c, v)
     to_nodes(lambda peer: v.r_out.at[peer], v.r_all.at[node], v.rb_send, v.rb_recv)
     v.r_all[node] = v.r_out[node]
 
-    settle(v.e1_out.at[most], v.e1_in.at[most], v.e1_recv)
-    transform(c, v)
-
-    combiner = me // c.share
-    slot = node * c.share + lax.rem(me, c.share)
-
-    def send_modes(k, carry):
-        peer = lax.rem(me + k, span)
-        where = {"node": combiner, "span": peer}
-        start(remote(v.e2_out.at[peer], v.e2_in.at[slot], v.e2_send, v.e2_recv, where))
-        return carry
-
-    lax.fori_loop(1, span, send_modes, 0)
-    own = remote(v.e2_out.at[me], v.e2_in.at[slot], v.e2_own, v.e2_recv, {"node": combiner})
-
-    @pl.when(combiner != node)
-    def _():
-        start(own)
-
-    @pl.when(combiner == node)
-    def _():
-        start(pltpu.make_async_copy(v.e2_out.at[me], v.e2_in.at[slot], v.e2_recv))
-
-    settle(v.r_out.at[some], v.r_all.at[some], v.rb_recv)
-    known_part(c, v)
-
     settle(v.e2_out, v.e2_in, v.e2_recv)
     blend_modes(c, v)
     to_nodes(lambda peer: v.a_out.at[peer], v.a_all.at[node], v.ab_send, v.ab_recv)
     v.a_all[node] = v.a_out[node]
+    settle(v.r_out.at[some], v.r_all.at[some], v.rb_recv)
+    known_part(c, v)
     settle(v.a_out.at[some], v.a_all.at[some], v.ab_recv)
     finish(c, v, out_ref)
 
@@ -402,7 +416,7 @@
         settle(v.e2_out.at[0], v.e2_in.at[0], v.e2_own)
 
 
-def local(nodes, span, iterate, start_field, spanwise_velocity, eigen_basis, inverse_basis, decay_rates):
+def local(nodes, span, chips, iterate, start_field, spanwise_velocity, eigen_basis, inverse_basis, decay_rates):
     ny, modes = iterate.shape[2], iterate.shape[3]
     lines = spanwise_velocity.shape[1]
     share, rows = span // nodes, ny // nodes
@@ -419,7 +433,7 @@
         jnp.asarray(turns),
     ]
     sizes = dict(
-        nodes=nodes, span=span, lines=lines, modes=modes, ny=ny, nz=span * modes, share=share,
+        nodes=nodes, span=span, chips=chips, lines=lines, modes=modes, ny=ny, nz=span * modes, share=share,
         rows=rows, group=math.gcd(16, span), chunk_rows=HALF // 4,
         quadrature=quadrature, shifts=shifts,
     )
@@ -438,7 +452,7 @@
         lines_f32=pltpu.VMEM((span, 8, LANES), F32), e1_out=lines_bf, e1_in=lines_bf,
         r_in=parts_f32, r_out=parts_f32, r_all=parts_f32,
         e2_out=lines_bf, e2_in=lines_bf, a_out=parts_bf, a_all=parts_bf,
-        load=dma((len(INPUTS),)),
+        load=dma((len(INPUTS),)), ready=pltpu.SemaphoreType.REGULAR,
         e1_send=dma, e1_recv=dma, rt_send=dma, rt_recv=dma, rb_send=dma, rb_recv=dma,
         e2_send=dma, e2_own=dma, e2_recv=dma, ab_send=dma, ab_recv=dma,
     )
@@ -457,7 +471,7 @@
 
 def solution(mesh):
     return jax.shard_map(
-        functools.partial(local, mesh.shape["node"], mesh.shape["span"]),
+        functools.partial(local, mesh.shape["node"], mesh.shape["span"], RING),
         mesh=mesh,
         in_specs=(
             P("node", None, None, "span"),

time: 66.2 us -> 67.2 us (1.015)
  the two profiles are of different devices: /device:TPU:24 before, /device:TPU:47 now
where the time goes in v3:
time: 67.2 us; the launch traced here: 67 us
  Pallas kernels  64.1 us (95%)
  local copies, waits for them, and re-layouts  2.92 us (4%)
    pallas_call x1, Pallas kernels, local(): pl.pallas_call(functools.partial(sweep, sizes, tuple(scratch)), out_shape...  64.1 us
    unnamed x1, local copies, waits for them, and re-layouts  1.65 us

profile of v3, /device:TPU:47, one launch (start us, length us, event | category | flops | bytes accessed | tf_op | source)
XLA Modules:
  0.0 67.0 jit_solution(4955976016409428437)
XLA Ops:
  0.0 1.3 %broadcast_in_dim.6.refs_5_ = f32[1,576]{1,0:T(1,128)} reshape(f32[576]{0:T(1024)} %param.13) | data formatting | bytes 4608 | tf_op jit(solution)/shard_map/broadcast_in_dim | solution.py:431
  1.3 64.1 %shard_map.82 = f32[2,48,576]{2,1,0:T(8,128)} custom-call(f32[2,48,576]{2,1,0:T(8,128)} %bitcast.9, f32[2,48,576]{2,1,0:T(8,128)} %bitcast.10, f32[216,128]{1,0:T(8,128)} %bitcast.11, f32[576,576]{1,0:T(8,128)} %refs_3_.1, f32[576,576]{1,0:T(8,128)} %refs_4_.1, f32[1,576]{1,0:T(1,128)} %broadcast_in_dim.6.refs_5_, bf16[896,256]{1,0:T(8,128)(2,1)} %constant.4.clone.refs_6_, ...), custom_call_target="tpu_custom_call" | custom-call | tf_op jit(solution)/shard_map/pallas_call | solution.py:459
  65.4 1.7 %copy.10 = f32[1,2,576,48]{2,3,1,0:T(8,128)} copy(f32[1,2,576,48]{2,3,1,0:T(8,128)} %bitcast.8) | data formatting | bytes 442368

commit v4 on v3

--- a/solution.py
+++ b/solution.py
@@ -321,8 +321,15 @@
         lax.fori_loop(0, chips - 1, step, 0)
         ring(chip, False)
 
+    def each_neighbour(act):
+        def step(k, carry):
+            act(lax.rem(me + k, span))
+            return carry
+
+        lax.fori_loop(1, span, step, 0)
+
     barrier = pltpu.get_barrier_semaphore()
-    each_peer(lambda peer: greet(barrier, {"span": peer}))
+    each_neighbour(lambda peer: greet(barrier, {"span": peer}))
     for k in range(1, nodes):
         greet(barrier, {"node": lax.rem(node + k, nodes)})
 
@@ -354,7 +361,7 @@
     def send_lines(peer):
         start(remote(v.e1_out.at[peer], v.e1_in.at[me], v.e1_send, v.e1_recv, {"span": peer}))
 
-    each_peer(send_lines)
+    each_neighbour(send_lines)
 
     def to_nodes(source, target, send_sem, recv_sem):
         for k in range(1, nodes):

time: 67.2 us -> 64.2 us (0.955)
  the two profiles are of different devices: /device:TPU:47 before, /device:TPU:1 now
where the time goes in v4:
time: 64.2 us; the launch traced here: 64 us
  Pallas kernels  61.1 us (95%)
  local copies, waits for them, and re-layouts  2.92 us (5%)
    pallas_call x1, Pallas kernels, local(): pl.pallas_call(functools.partial(sweep, sizes, tuple(scratch)), out_shape...  61.1 us
    unnamed x1, local copies, waits for them, and re-layouts  1.65 us

profile of v4, /device:TPU:1, one launch (start us, length us, event | category | flops | bytes accessed | tf_op | source)
XLA Modules:
  0.0 64.0 jit_solution(14110479577859909773)
XLA Ops:
  0.0 1.3 %broadcast_in_dim.6.refs_5_ = f32[1,576]{1,0:T(1,128)} reshape(f32[576]{0:T(1024)} %param.13) | data formatting | bytes 4608 | tf_op jit(solution)/shard_map/broadcast_in_dim | solution.py:438
  1.3 61.1 %shard_map.82 = f32[2,48,576]{2,1,0:T(8,128)} custom-call(f32[2,48,576]{2,1,0:T(8,128)} %bitcast.9, f32[2,48,576]{2,1,0:T(8,128)} %bitcast.10, f32[216,128]{1,0:T(8,128)} %bitcast.11, f32[576,576]{1,0:T(8,128)} %refs_3_.1, f32[576,576]{1,0:T(8,128)} %refs_4_.1, f32[1,576]{1,0:T(1,128)} %broadcast_in_dim.6.refs_5_, bf16[896,256]{1,0:T(8,128)(2,1)} %constant.4.clone.refs_6_, ...), custom_call_target="tpu_custom_call" | custom-call | tf_op jit(solution)/shard_map/pallas_call | solution.py:466
  62.4 1.7 %copy.10 = f32[1,2,576,48]{2,3,1,0:T(8,128)} copy(f32[1,2,576,48]{2,3,1,0:T(8,128)} %bitcast.8) | data formatting | bytes 442368
